TPU v7x, 256 devices: a whole 4x4x8 slice. The times are simulated.
256 devices in a mesh: qrow: 32 (over z_hi, y, core), kcol: 8 (over z_lo, x).
Axes of the slice: x: 4, y: 4, z: 8 (z_hi: 4, z_lo: 2; z = z_hi * 2 + z_lo), core: 2. Of those that a mesh axis runs over, the one named last changes fastest.
Arguments:
- queries: bfloat16 [32768, 256], P(('qrow', 'kcol'))
- keys: bfloat16 [32768, 128], P(('qrow', 'kcol'))
- values: bfloat16 [32768, 128], P(('qrow', 'kcol'))
- out_grad: bfloat16 [32768, 256], P(('qrow', 'kcol'))
- outputs: bfloat16 [32768, 256], P(('qrow', 'kcol')), as said below
- log_norm: float32 [2, 32768], P(None, ('qrow', 'kcol')), as said below
- perm_blocks: int32 [256], replicated, may hold values from 0 to 255, as said below
- doc_bounds: int32 [16], replicated, may hold values from 0 to 32767, as said below
- block_map: int32 [256, 256], replicated, may hold values from 0 to 1, as said below
Outputs:
- grad_query: float32 [32768, 256], P(('qrow', 'kcol'))
- grad_key: float32 [32768, 128], P(('qrow', 'kcol'))
- grad_value: float32 [32768, 128], P(('qrow', 'kcol'))
Inputs may be any that keep to these rules, and one draw needn't show every extreme that they name: `perm_blocks`: every sequence block appears once. `doc_bounds`: strictly increasing, the first entry 0. `block_map`: an entry is 1 exactly where some token of the first block may attend some token of the second under the causal document mask, else 0. `log_norm`: for each head and query, the log of the sum of exp(scores) over the keys it is allowed, with the given queries and keys. `outputs`: the forward attention output of the given queries, keys and values under the same mask, rounded to bfloat16.
All inputs are finite; a program needn't handle non-finite values.
Results may differ from a plain program's by a relative error of at most 0.0029.
Values may be sent and summed in bfloat16 or wider, within the bound.
No kernel may reach another device: no remote copies, remote signals or barrier semaphores. Data moves between devices by JAX's collectives and lax.ppermute only.
A program may use at most 128 MiB of HBM per device.

v0:
```python
import math

import jax
import jax.numpy as jnp
from jax import lax
from jax.sharding import PartitionSpec as P


def doc_starts(doc_bounds, positions):
    found = jnp.where(doc_bounds[None, :] <= positions[:, None], doc_bounds[None, :], 0)
    return jnp.max(found, axis=1)


def block_positions(perm_blocks, block_ids, block_len):
    offsets = jnp.arange(block_len, dtype=jnp.int32)
    return (perm_blocks[block_ids][:, None] * block_len + offsets[None, :]).reshape(-1)


def tile_grads(
    query_all,
    grad_all,
    norm_all,
    delta_all,
    key_all,
    value_all,
    query_ids,
    key_ids,
    perm_blocks,
    doc_bounds,
    block_map,
    block_len,
):
    head_count = norm_all.shape[0]
    head_width = key_all.shape[1]
    score_scale = head_width ** (-0.5)
    query_pos = block_positions(perm_blocks, query_ids, block_len)
    key_pos = block_positions(perm_blocks, key_ids, block_len)
    starts = doc_starts(doc_bounds, query_pos)
    tile_table = block_map[perm_blocks[query_ids]][:, perm_blocks[key_ids]]
    row_table = jnp.repeat(tile_table, block_len, axis=0)
    query_count = query_all.shape[0]
    key_count = key_all.shape[0]
    block_rows = math.gcd(query_count, 512)
    steps_count = query_count // block_rows
    slices = (
        query_all.reshape(steps_count, block_rows, head_count, head_width),
        grad_all.reshape(steps_count, block_rows, head_count, head_width),
        norm_all.reshape(head_count, steps_count, block_rows).transpose(1, 0, 2),
        delta_all.reshape(head_count, steps_count, block_rows).transpose(1, 0, 2),
        query_pos.reshape(steps_count, block_rows),
        starts.reshape(steps_count, block_rows),
        row_table.reshape(steps_count, block_rows, row_table.shape[1]),
    )

    def block_step(state, pieces):
        query_part, grad_part, norm_part, delta_part, pos_part, start_part, table_part = pieces
        key_table = jnp.repeat(table_part, block_len, axis=1)
        allowed = (
            (start_part[:, None] <= key_pos[None, :])
            & (key_pos[None, :] <= pos_part[:, None])
            & (key_table == 1)
        )
        grad_key, grad_value = state
        scores = (
            jnp.einsum("qhd,kd->hqk", query_part, key_all, preferred_element_type=jnp.float32)
            * score_scale
        )
        weights = jnp.where(allowed[None], jnp.exp(scores - norm_part[:, :, None]), 0.0)
        weights_b = weights.astype(jnp.bfloat16)
        grad_value = grad_value + jnp.einsum(
            "hqk,qhd->kd", weights_b, grad_part, preferred_element_type=jnp.float32
        )
        dprob = jnp.einsum("qhd,kd->hqk", grad_part, value_all, preferred_element_type=jnp.float32)
        dscore = (weights * (dprob - delta_part[:, :, None]) * score_scale).astype(jnp.bfloat16)
        grad_query = jnp.einsum("hqk,kd->qhd", dscore, key_all, preferred_element_type=jnp.float32)
        grad_key = grad_key + jnp.einsum(
            "hqk,qhd->kd", dscore, query_part, preferred_element_type=jnp.float32
        )
        grad_query, grad_key, grad_value = (
            grad_query.reshape(block_rows, head_count * head_width),
            grad_key,
            grad_value,
        )
        return ((grad_key, grad_value), grad_query)

    zeros_keys = jnp.zeros((key_count, head_width), jnp.float32)
    (grad_key, grad_value), grad_blocks = lax.scan(block_step, (zeros_keys, zeros_keys), slices)
    return (grad_blocks.reshape(query_count, head_count * head_width), grad_key, grad_value)


def body(queries, keys, values, out_grad, outputs, log_norm, perm_blocks, doc_bounds, block_map):
    block_len = queries.shape[0]
    head_count = log_norm.shape[0]
    head_width = keys.shape[1]
    rows_total = lax.axis_size("qrow")
    cols_total = lax.axis_size("kcol")
    row_index = lax.axis_index("qrow")
    col_index = lax.axis_index("kcol")
    products = (out_grad.astype(jnp.float32) * outputs.astype(jnp.float32)).reshape(
        block_len, head_count, head_width
    )
    row_delta = jnp.sum(products, axis=2).T
    column_ids = jnp.arange(rows_total, dtype=jnp.int32) * cols_total + col_index
    row_block_ids = row_index * cols_total + jnp.arange(cols_total, dtype=jnp.int32)
    query_all, grad_all = (
        lax.all_gather(queries, "qrow", axis=0, tiled=True),
        lax.all_gather(out_grad, "qrow", axis=0, tiled=True),
    )
    norm_all, delta_all = (
        lax.all_gather(log_norm, "qrow", axis=1, tiled=True),
        lax.all_gather(row_delta, "qrow", axis=1, tiled=True),
    )
    key_all, value_all = (
        lax.all_gather(keys, "kcol", axis=0, tiled=True),
        lax.all_gather(values, "kcol", axis=0, tiled=True),
    )
    grad_query, grad_key, grad_value = tile_grads(
        query_all,
        grad_all,
        norm_all,
        delta_all,
        key_all,
        value_all,
        column_ids,
        row_block_ids,
        perm_blocks,
        doc_bounds,
        block_map,
        block_len,
    )
    query_out = lax.psum_scatter(grad_query, "qrow", scatter_dimension=0, tiled=True)
    key_out, value_out = (
        lax.psum_scatter(grad_key, "kcol", scatter_dimension=0, tiled=True),
        lax.psum_scatter(grad_value, "kcol", scatter_dimension=0, tiled=True),
    )
    return (query_out, key_out, value_out)


def solution(mesh):
    return jax.shard_map(
        body,
        mesh=mesh,
        in_specs=(
            P(("qrow", "kcol"), None),
            P(("qrow", "kcol"), None),
            P(("qrow", "kcol"), None),
            P(("qrow", "kcol"), None),
            P(("qrow", "kcol"), None),
            P(None, ("qrow", "kcol")),
            P(),
            P(),
            P(),
        ),
        out_specs=(P(("qrow", "kcol"), None), P(("qrow", "kcol"), None), P(("qrow", "kcol"), None)),
        check_vma=False,
    )
```

profile of v0, /device:TPU:2, one launch (start us, length us, event | category | flops | bytes accessed | tf_op | source)
XLA Modules:
  0.0 465.3 jit_solution(1783569635981290612)
XLA Ops:
  16.0 66.4 %all_gather.23 = f32[2,4096]{0,1:T(8,128)S(1)} all-gather(f32[2,128]{0,1:T(8,128)S(1)} %bitcast.143), channel_id=1, replica_groups=mesh['qrow'=32,'kcol'=8] {'qrow'}, dimensions={1}, use_global_device_ids=true | all-gather | bytes 33792 | tf_op jit(solution)/shard_map/all_gather | solution.py:111
  83.0 39.2 %all_gather.20 = f32[2,4096]{1,0:T(2,128)S(1)} all-gather(f32[2,128]{1,0:T(2,128)S(1)} %copy-done.3), channel_id=1, replica_groups=mesh['qrow'=32,'kcol'=8] {'qrow'}, dimensions={1}, use_global_device_ids=true | all-gather | bytes 33792 | tf_op jit(solution)/shard_map/all_gather | solution.py:110
  122.2 24.2 %all_gather.19 = bf16[1024,128]{0,1:T(8,128)(2,1)S(1)} all-gather(bf16[128,128]{0,1:T(8,128)(2,1)S(1)} %copy.54), channel_id=1, replica_groups=mesh['qrow'=32,'kcol'=8] {'kcol'}, dimensions={0}, use_global_device_ids=true | all-gather | bytes 294912 | tf_op jit(solution)/shard_map/all_gather | solution.py:114
  146.4 27.1 %all_gather.22 = bf16[1024,128]{1,0:T(8,128)(2,1)S(1)} all-gather(bf16[128,128]{1,0:T(8,128)(2,1)} %param.13), channel_id=1, replica_groups=mesh['qrow'=32,'kcol'=8] {'kcol'}, dimensions={0}, use_global_device_ids=true | all-gather | bytes 294912 | tf_op jit(solution)/shard_map/all_gather | solution.py:115
  173.5 4.0 reshape.245
  177.5 4.0 reshape.246
  183.0 93.3 %while.15 = (s32[]{:T(128)}, f32[1024,128]{1,0:T(8,128)S(1)}, f32[1024,128]{1,0:T(8,128)S(1)}, f32[8,512,256]{2,1,0:T(8,128)}, s32[8,512]{1,0:T(8,128)S(1)}, /*i...) while((s32[]{:T(128)}, f32[1024,128]{1,0:T(8,128)S(1)}, ...), condition=%wide.region_3.4_spmd.clone, body=%wide.region_2.3_spmd.clone.sunk | while | flops 1356338176 | bytes 29171932 | solution.py:87
  184.1 1.6 broadcast_in_dim.89
  188.5 1.6 fusion.54
  190.1 1.9 fusion.52
  195.8 1.6 broadcast_in_dim.89
  200.2 1.6 fusion.54
  201.8 1.9 fusion.52
  211.8 1.6 fusion.54
  213.4 1.9 fusion.52
  219.1 1.6 broadcast_in_dim.89
  223.5 1.6 fusion.54
  225.1 1.9 fusion.52
  230.8 1.6 broadcast_in_dim.89
  235.2 1.6 fusion.54
  236.8 1.9 fusion.52
  242.5 1.6 broadcast_in_dim.89
  246.8 1.6 fusion.54
  248.5 1.9 fusion.52
  254.1 1.6 broadcast_in_dim.89
  258.5 1.6 fusion.54
  260.1 1.9 fusion.52
  270.2 1.6 fusion.54
  271.8 1.9 fusion.52
  278.4 32.6 %reduce-scatter.6.cloned.1.call-done = f32[128,128]{1,0:T(8,128)} async-done(((f32[1024,128]{1,0:T(8,128)}), f32[128,128]{1,0:T(8,128)}) %reduce-scatter.6.cloned.1.call-update) | async-done | bytes 65552 | tf_op jit(solution)/shard_map/reduce_scatter | solution.py:133
  310.9 42.2 %reduce-scatter.8.cloned.1.call-done = f32[128,128]{1,0:T(8,128)} async-done(((f32[1024,128]{1,0:T(8,128)}), f32[128,128]{1,0:T(8,128)}) %reduce-scatter.8.cloned.1.call-update) | async-done | bytes 65552 | tf_op jit(solution)/shard_map/reduce_scatter | solution.py:134
  353.1 105.7 %reduce-scatter.4.cloned.1.call-done = f32[128,256]{1,0:T(8,128)} async-done(((f32[4096,256]{1,0:T(8,128)}), f32[128,256]{1,0:T(8,128)}) %reduce-scatter.4.cloned.1.call-update) | async-done | bytes 131088 | tf_op jit(solution)/shard_map/reduce_scatter | solution.py:131
  (142 shorter events, 68.1 us)
Async XLA Ops:
  7.2 6.3 %copy-start = (s32[256,256]{1,0:T(8,128)S(1)}, s32[256,256]{1,0:T(8,128)}, u32[]{:S(2)}) copy-start(s32[256,256]{1,0:T(8,128)} %param.19) | copy-start | bytes 786436
  7.2 75.8 %copy-start.3 = (f32[2,128]{1,0:T(2,128)S(1)}, f32[2,128]{1,0:T(2,128)}, u32[]{:S(2)}) copy-start(f32[2,128]{1,0:T(2,128)} %param.16) | copy-start | bytes 3076
  7.2 166.3 %all-gather.3.cloned.1.call-start = ((), (), s32[]{:S(2)}) async-start(), calls=%async_computation.3 | async-start | bytes 2162688 | tf_op jit(solution)/shard_map/all_gather | solution.py:106
  7.9 169.6 %all-gather.5.cloned.1.call-start = ((), (), s32[]{:S(2)}) async-start(), calls=%async_computation.4 | async-start | bytes 2162688 | tf_op jit(solution)/shard_map/all_gather | solution.py:107
  8.7 302.3 %reduce-scatter.6.cloned.1.call-start = ((), (), s32[]{:S(2)}) async-start(), calls=%async_computation.6 | async-start | bytes 589824 | tf_op jit(solution)/shard_map/reduce_scatter | solution.py:133
  276.4 0.8 copy-start.1
  276.4 1.0 copy-start.2
  277.2 75.9 %reduce-scatter.8.cloned.1.call-start = ((), (), s32[]{:S(2)}) async-start(), calls=%async_computation.7 | async-start | bytes 589824 | tf_op jit(solution)/shard_map/reduce_scatter | solution.py:134
  277.8 181.0 %reduce-scatter.4.cloned.1.call-start = ((), (), s32[]{:S(2)}) async-start(), calls=%async_computation.5 | async-start | bytes 4325376 | tf_op jit(solution)/shard_map/reduce_scatter | solution.py:131
Sparse Core Ops, SparseCore 0:
  10.6 61.8 all-gather.2
  75.0 52.2 all-gather.4
  277.3 33.5 reduce-scatter.5
  314.0 39.0 reduce-scatter.7
  357.5 101.2 reduce-scatter.3
where the time goes:
time: 466 us; the launch traced here: 465 us
  waiting for transfers between devices  183 us (39%)
  blocking collectives  157 us (34%)
  local copies, waits for them, and re-layouts  48.6 us (10%)
  matrix products  46.7 us (10%)
  other arithmetic  15.7 us (3%)
  between operations  13.9 us (3%)
    reduce_scatter x1, waiting for transfers between devices, body(): lax.psum_scatter(grad_query, 'qrow', scatter_dimension=0, tiled=True)  106 us
    all_gather x1, blocking collectives, body(): lax.all_gather(row_delta, 'qrow', axis=1, tiled=True)  66.4 us
    reduce_scatter x1, waiting for transfers between devices, body(): lax.psum_scatter(grad_value, 'kcol', scatter_dimension=0, tiled=True)  42.2 us
    all_gather x1, blocking collectives, body(): lax.all_gather(log_norm, 'qrow', axis=1, tiled=True)  39.2 us
    reduce_scatter x1, waiting for transfers between devices, body(): lax.psum_scatter(grad_key, 'kcol', scatter_dimension=0, tiled=True)  32.6 us
    all_gather x1, blocking collectives, body(): lax.all_gather(values, 'kcol', axis=0, tiled=True)  27.1 us
    all_gather x1, blocking collectives, body(): lax.all_gather(keys, 'kcol', axis=0, tiled=True)  24.2 us
    dot_general x8, matrix products, block_step(): jnp.einsum('qhd,kd->hqk', grad_part, value_all, preferred_element_type=jn...  14.9 us
  transfers between devices with their start and end apart: 5, of which 3 were waited for; matrix products, arithmetic and copies ran while one was open for 3% of the time, Pallas kernels for 0%

commit v1 on v0

v1 whole, which is shorter than its diff:
```python
import jax
import jax.numpy as jnp
import numpy as np
from jax import lax
from jax.experimental import pallas as pl
from jax.experimental.pallas import tpu as pltpu
from jax.sharding import PartitionSpec as P

AXES = ("qrow", "kcol")
LOG2E = 1.4426950408889634
TOK = 128
AUX = 16
QROWS = 4 * TOK + AUX
GROUP = 16


def coords(i):
    return (i // 64) * 2 + (i // 4) % 2, (i // 16) % 4, (i // 8) % 2, i % 4


def index(z, y, core, x):
    return (((z // 2) * 4 + y) * 2 + core) * 8 + (z % 2) * 4 + x


def pair4(i, flip):
    return 3 - i if flip else i ^ 1


def pair_z(z, y, c, x):
    return (z ^ 1 if c == 0 else (z + (1 if z % 2 else -1)) % 8), y, c, x


def pair_x1(z, y, c, x):
    return z, y, c, pair4(x, c == 1)


def pair_x2(z, y, c, x):
    return z, y, c, pair4(x, c == 0)


def pair_core(z, y, c, x):
    return z, y, 1 - c, x


def pair_z1(z, y, c, x):
    return 2 * pair4(z // 2, c == 1) + z % 2, y, c, x


def pair_z2(z, y, c, x):
    return 2 * pair4(z // 2, c == 0) + z % 2, y, c, x


def pair_y1(z, y, c, x):
    return z, pair4(y, c == 1), c, x


def pair_y2(z, y, c, x):
    return z, pair4(y, c == 0), c, x


def partners(pair):
    return np.array([index(*pair(*coords(i))) for i in range(256)])


def slot_table(pairs):
    table = np.arange(256)[:, None]
    for pair in pairs:
        table = np.concatenate([table, table[partners(pair)]], axis=1)
    return table


def swap(value, pair):
    to = partners(pair)
    return lax.ppermute(value, AXES, [(i, int(to[i])) for i in range(256)])


def prep_kernel(q_ref, g_ref, o_ref, n_ref, k_ref, v_ref, qpay_ref, kvpay_ref):
    rows = [n_ref[0:1, :], n_ref[1:2, :]]
    for head in range(2):
        cols = slice(head * TOK, (head + 1) * TOK)
        qpay_ref[head * TOK : (head + 1) * TOK, :] = q_ref[:, cols]
        qpay_ref[(2 + head) * TOK : (3 + head) * TOK, :] = g_ref[:, cols]
        product = g_ref[:, cols].astype(jnp.float32) * o_ref[:, cols].astype(jnp.float32)
        rows.append(jnp.sum(product.T, axis=0, keepdims=True))
    exact = jnp.concatenate(rows, axis=0)
    high = exact.astype(jnp.bfloat16).astype(jnp.float32)
    rest = exact - high
    mid = rest.astype(jnp.bfloat16).astype(jnp.float32)
    low = rest - mid
    parts = jnp.concatenate([high, mid, low, jnp.zeros_like(low)], axis=0)
    qpay_ref[4 * TOK :, :] = parts.astype(jnp.bfloat16)
    kvpay_ref[0:TOK, :] = k_ref[...]
    kvpay_ref[TOK:, :] = v_ref[...]


def list_kernel(perm_ref, bounds_ref, ids_ref, list_ref, base_ref, rows_ref):
    lane = lax.broadcasted_iota(jnp.int32, (1, TOK), 1)
    for slot in range(GROUP):
        base_ref[slot] = perm_ref[ids_ref[GROUP + slot]] * TOK
        first = perm_ref[ids_ref[slot]] * TOK
        position = first + lane
        start = jnp.zeros((1, TOK), jnp.int32)
        first_start = jnp.int32(0)
        for doc in range(16):
            bound = bounds_ref[doc]
            start = jnp.where(position >= bound, bound, start)
            first_start = jnp.where(first >= bound, bound, first_start)
        base_ref[GROUP + 1 + slot] = first
        base_ref[2 * GROUP + 1 + slot] = first_start
        rows_ref[slot, 0:1, :] = start
        rows_ref[slot, 1:2, :] = position
    base_ref[GROUP] = jnp.int32(-(1 << 20))

    def outer(ks, count):
        key_base = base_ref[ks]

        def inner(qs, count):
            active = (key_base <= base_ref[GROUP + 1 + qs]) & (
                base_ref[2 * GROUP + 1 + qs] <= key_base + (TOK - 1)
            )
            list_ref[1 + count] = qs + GROUP * ks
            return count + active.astype(jnp.int32)

        return lax.fori_loop(0, GROUP, inner, count, unroll=True)

    count = lax.fori_loop(0, GROUP, outer, jnp.int32(0))
    list_ref[0] = count
    list_ref[1 + count] = jnp.int32(GROUP * GROUP)


NT = (((1,), (1,)), ((), ()))


def main_kernel(list_ref, base_ref, rows_ref, qa_ref, qb_ref, kv_ref, dqa_ref, dqb_ref, ga_ref, gb_ref, dq, dkv, aux, kt):
    half = GROUP // 2
    scale = TOK ** (-0.5)
    dq[...] = jnp.zeros_like(dq)
    dkv[...] = jnp.zeros_like(dkv)
    for slot in range(GROUP):
        q_ref = qa_ref if slot < half else qb_ref
        parts = q_ref[slot % half, 4 * TOK :, :].astype(jnp.float32)
        exact = (parts[8:12] + parts[4:8]) + parts[0:4]
        for head in range(2):
            cols = slice(head * TOK, (head + 1) * TOK)
            aux[slot, 0:1, cols] = exact[head : head + 1] * LOG2E
            aux[slot, 1:2, cols] = exact[2 + head : 3 + head]
        kt[slot] = kv_ref[slot, 0:TOK, :].T
    sub = lax.broadcasted_iota(jnp.int32, (TOK, TOK), 0)

    def tile(q_ref, qs, ql, ks):
        kl = ks & (GROUP - 1)
        base = base_ref[ks]
        q = q_ref[ql, 0 : 2 * TOK, :]
        g = q_ref[ql, 2 * TOK : 4 * TOK, :]
        k = kv_ref[kl, 0:TOK, :]
        v = kv_ref[kl, TOK:, :]
        scores = lax.dot_general(k, q, NT, preferred_element_type=jnp.float32)
        dprob = lax.dot_general(v, g, NT, preferred_element_type=jnp.float32)
        allowed = (sub >= rows_ref[qs, 0:1, :] - base) & (sub <= rows_ref[qs, 1:2, :] - base)
        allowed = jnp.concatenate([allowed, allowed], axis=1)
        weights = jnp.where(allowed, jnp.exp2(scores * (scale * LOG2E) - aux[qs, 0:1, :]), 0.0)
        dscore = (weights * (dprob - aux[qs, 1:2, :]) * scale).astype(jnp.bfloat16)
        weights_b = weights.astype(jnp.bfloat16)
        dv = jnp.dot(weights_b, g, preferred_element_type=jnp.float32)
        dk = jnp.dot(dscore, q, preferred_element_type=jnp.float32)
        dqt = jnp.dot(kt[kl], dscore, preferred_element_type=jnp.float32)
        return kl, dv, dk, dqt

    def step(i, carry):
        entry = list_ref[1 + i]
        qs, ks = entry & (GROUP - 1), entry >> 4

        def run(q_ref, ql):
            kl, dv, dk, dqt = tile(q_ref, qs, ql, ks)
            dkv[kl, 0:TOK, :] += dk
            dkv[kl, TOK:, :] += dv
            dq[qs] += dqt

        pl.when(qs < half)(lambda: run(qa_ref, qs))
        pl.when(qs >= half)(lambda: run(qb_ref, qs - half))
        return carry

    lax.fori_loop(0, list_ref[0], step, 0)
    dqa_ref[...] = dq[0:half]
    dqb_ref[...] = dq[half:]
    ga_ref[...] = dkv[0:half]
    gb_ref[...] = dkv[half:].astype(jnp.bfloat16)


def spec(space=pltpu.VMEM):
    return pl.BlockSpec(memory_space=space)


def body(queries, keys, values, out_grad, outputs, log_norm, perm_blocks, doc_bounds, block_map):
    del block_map
    half = GROUP // 2
    me = lax.axis_index("qrow") * lax.axis_size("kcol") + lax.axis_index("kcol")
    ids = jnp.asarray(
        np.concatenate(
            [slot_table([pair_z, pair_x1, pair_x2, pair_core]), slot_table([pair_z1, pair_z2, pair_y1, pair_y2])], axis=1
        ).astype(np.int32)
    )[me]
    params = pltpu.CompilerParams(vmem_limit_bytes=48 * 1024 * 1024)
    q1, kv1 = pl.pallas_call(
        prep_kernel,
        out_shape=(
            jax.ShapeDtypeStruct((QROWS, TOK), jnp.bfloat16),
            jax.ShapeDtypeStruct((2 * TOK, TOK), jnp.bfloat16),
        ),
        in_specs=[spec()] * 6,
        out_specs=(spec(), spec()),
        compiler_params=params,
        name="prep",
    )(queries, out_grad, outputs, log_norm, keys, values)
    tiles, bases, rows = pl.pallas_call(
        list_kernel,
        out_shape=(
            jax.ShapeDtypeStruct((GROUP * GROUP + 8,), jnp.int32),
            jax.ShapeDtypeStruct((64,), jnp.int32),
            jax.ShapeDtypeStruct((GROUP, 8, TOK), jnp.int32),
        ),
        in_specs=[spec(pltpu.SMEM)] * 3,
        out_specs=(spec(pltpu.SMEM), spec(pltpu.SMEM), spec()),
        compiler_params=params,
        name="tiles",
    )(perm_blocks, doc_bounds, ids)

    q2 = jnp.concatenate([q1[None], swap(q1, pair_z)[None]])
    kv2 = jnp.concatenate([kv1[None], swap(kv1, pair_z1)[None]])
    q4 = jnp.concatenate([q2, swap(q2, pair_x1)])
    kv4 = jnp.concatenate([kv2, swap(kv2, pair_z2)])
    q8 = jnp.concatenate([q4, swap(q4, pair_x2)])
    kv8 = jnp.concatenate([kv4, swap(kv4, pair_y1)])
    other8 = swap(q8, pair_core)
    kv16 = jnp.concatenate([kv8, swap(kv8, pair_y2)])

    dqa, dqb, ga, gb = pl.pallas_call(
        main_kernel,
        out_shape=(
            jax.ShapeDtypeStruct((half, TOK, 2 * TOK), jnp.float32),
            jax.ShapeDtypeStruct((half, TOK, 2 * TOK), jnp.float32),
            jax.ShapeDtypeStruct((half, 2 * TOK, TOK), jnp.float32),
            jax.ShapeDtypeStruct((half, 2 * TOK, TOK), jnp.bfloat16),
        ),
        in_specs=[spec(pltpu.SMEM)] * 2 + [spec()] * 4,
        out_specs=(spec(),) * 4,
        scratch_shapes=[
            pltpu.VMEM((GROUP, TOK, 2 * TOK), jnp.float32),
            pltpu.VMEM((GROUP, 2 * TOK, TOK), jnp.float32),
            pltpu.VMEM((GROUP, 8, 2 * TOK), jnp.float32),
            pltpu.VMEM((GROUP, TOK, TOK), jnp.bfloat16),
        ],
        compiler_params=params,
        cost_estimate=pl.CostEstimate(flops=10**9, bytes_accessed=10**7, transcendentals=10**6),
        name="main",
    )(tiles, bases, rows, q8, other8, kv16)

    dq8 = dqa + swap(dqb, pair_core)
    g8 = ga + swap(gb, pair_y2).astype(jnp.float32)
    dq4 = dq8[:4] + swap(dq8[4:].astype(jnp.bfloat16), pair_x2).astype(jnp.float32)
    g4 = g8[:4] + swap(g8[4:].astype(jnp.bfloat16), pair_y1).astype(jnp.float32)
    dq2 = dq4[:2] + swap(dq4[2:].astype(jnp.bfloat16), pair_x1).astype(jnp.float32)
    g2 = g4[:2] + swap(g4[2:], pair_z2)
    dq1 = dq2[0] + swap(dq2[1], pair_z)
    g1 = g2[0] + swap(g2[1], pair_z1)
    grad_query = dq1.reshape(TOK, 2, TOK).transpose(2, 1, 0).reshape(TOK, 2 * TOK)
    return grad_query, g1[:TOK], g1[TOK:]


def solution(mesh):
    rows, cols = P(AXES, None), P(None, AXES)
    return jax.shard_map(
        body,
        mesh=mesh,
        in_specs=(rows, rows, rows, rows, rows, cols, P(), P(), P()),
        out_specs=(rows, rows, rows),
        check_vma=False,
    )
```

time: 466 us -> 115 us (0.25)
  blocking collectives: 157 us -> 0 us
  waiting for transfers between devices: 183 us -> 53.4 us
  matrix products: 46.7 us -> 0 us
  local copies, waits for them, and re-layouts: 48.6 us -> 8.19 us
  starting transfers between devices: 0.19 us -> 40.5 us
  other arithmetic: 15.7 us -> 0.8 us
  between operations: 13.9 us -> 0.9 us
  Pallas kernels: 0 us -> 9.56 us
    reduce_scatter x3 -> x0, waiting for transfers between devices: 180 us -> none  [the longest x1 106 us: body(): lax.psum_scatter(grad_query, 'qrow', scatter_dimension=0, tiled=True)]
    all_gather x4 -> x0, blocking collectives: 157 us -> none  [the longest x1 66.4 us: body(): lax.all_gather(row_delta, 'qrow', axis=1, tiled=True)]
    ppermute x0 -> x16, waiting for transfers between devices: none -> 53.4 us  [swap(): return lax.ppermute(value, AXES, [(i, int(to[i])) for i in range(256)])]
    dot_general x40 -> x0, matrix products: 46.7 us -> none  [the longest x8 14.9 us: block_step(): jnp.einsum('qhd,kd->hqk', grad_part, value_all, preferred_element_type=jn...]
    ppermute x0 -> x16, starting transfers between devices: none -> 40.5 us  [swap(): return lax.ppermute(value, AXES, [(i, int(to[i])) for i in range(256)])]
    broadcast_in_dim x9 -> x0, local copies, waits for them, and re-layouts: 14.3 us -> none  [the longest x8 12.8 us: block_step(): key_table = jnp.repeat(table_part, block_len, axis=1)]
    dynamic_slice x16 -> x0, local copies, waits for them, and re-layouts: 11.2 us -> none  [tile_grads(): lax.scan(block_step, (zeros_keys, zeros_keys), slices)]
    pallas_call x0 -> x3, Pallas kernels: none -> 9.56 us  [the longest x1 7.14 us: body(): pl.pallas_call(main_kernel, out_shape=(jax.ShapeDtypeStruct((half, TOK, 2...]
  transfers between devices with their start and end apart: 5 -> 16, of which waited for: 3 -> 11; matrix products, arithmetic and copies ran while one was open for 3% -> 2% of each run, Pallas kernels for 0% -> 2%
where the time goes in v1:
time: 115 us; the launch traced here: 113 us
  waiting for transfers between devices  53.4 us (46%)
  starting transfers between devices  40.5 us (35%)
  Pallas kernels  9.56 us (8%)
  local copies, waits for them, and re-layouts  8.19 us (7%)
    ppermute x16, waiting for transfers between devices, swap(): return lax.ppermute(value, AXES, [(i, int(to[i])) for i in range(256)])  53.4 us
    ppermute x16, starting transfers between devices, swap(): return lax.ppermute(value, AXES, [(i, int(to[i])) for i in range(256)])  40.5 us
    pallas_call x1, Pallas kernels, body(): pl.pallas_call(main_kernel, out_shape=(jax.ShapeDtypeStruct((half, TOK, 2...  7.14 us
    unnamed x23, local copies, waits for them, and re-layouts  6.47 us
    pallas_call x1, Pallas kernels, body(): pl.pallas_call(list_kernel, out_shape=(jax.ShapeDtypeStruct((GROUP * GROU...  2.31 us
  transfers between devices with their start and end apart: 16, of which 11 were waited for; matrix products, arithmetic and copies ran while one was open for 2% of the time, Pallas kernels for 2%

profile of v1, /device:TPU:2, one launch (start us, length us, event | category | flops | bytes accessed | tf_op | source)
XLA Modules:
  0.0 113.3 jit_solution(17366547289157860316)
XLA Ops:
  0.6 0.8 copy-done
  1.5 0.8 copy-done.1
  2.3 0.8 copy-done.2
  3.2 0.8 copy-done.3
  3.9 0.8 copy-done.4
  5.5 2.0 %collective-permute-start = (bf16[528,128]{1,0:T(8,128)(2,1)S(1)}, bf16[528,128]{1,0:T(8,128)(2,1)S(1)}, u32[]{:S(2)}, u32[]{:S(2)}) collective-permute-start(bf16[528,128]{1,0:T(8,128)(2,1)S(1)} %get-tuple-element.15), channel_id=1, source_target_pairs={{0,4},{1,5},{2,6},{3,7},{4,0},{5,1},{6,2},{7,3},{8,204},{9,205},{1... | collective-permute-start | bytes 405512 | tf_op jit(solution)/shard_map/ppermute | solution.py:74
  7.5 3.1 %collective-permute-done = bf16[528,128]{1,0:T(8,128)(2,1)S(1)} collective-permute-done((bf16[528,128]{1,0:T(8,128)(2,1)S(1)}, bf16[528,128]{1,0:T(8,128)(2,1)S(1)}, u32[]{:S(2)}, u32[]{:S(2)}) %collective-permute-start) | collective-permute-done | bytes 135200 | tf_op jit(solution)/shard_map/ppermute | solution.py:74
  10.6 2.4 %collective-permute-start.1 = (bf16[2,528,128]{2,1,0:T(8,128)(2,1)S(1)}, bf16[2,528,128]{2,1,0:T(8,128)(2,1)S(1)}, u32[]{:S(2)}, u32[]{:S(2)}) collective-permute-start(bf16[2,528,128]{2,1,0:T(8,128)(2,1)S(1)} %pad_maximum_fusion.3), channel_id=1, source_target_pairs={{0,1},{1,0},{2,3},{3,2},{4,5},{5,4},{6,7},{7,6},{8,11},{9,10},{10,... | collective-permute-start | bytes 811016 | tf_op jit(solution)/shard_map/ppermute | solution.py:74
  13.0 4.4 %collective-permute-done.1 = bf16[2,528,128]{2,1,0:T(8,128)(2,1)S(1)} collective-permute-done((bf16[2,528,128]{2,1,0:T(8,128)(2,1)S(1)}, bf16[2,528,128]{2,1,0:T(8,128)(2,1)S(1)}, u32[]{:S(2)}, u32[]{:S(2)}) %collective-permute-start.1) | collective-permute-done | bytes 270368 | tf_op jit(solution)/shard_map/ppermute | solution.py:74
  17.5 1.3 %collective-permute-start.2 = (bf16[4,528,128]{2,1,0:T(8,128)(2,1)S(1)}, bf16[4,528,128]{2,1,0:T(8,128)(2,1)S(1)}, u32[]{:S(2)}, u32[]{:S(2)}) collective-permute-start(bf16[4,528,128]{2,1,0:T(8,128)(2,1)S(1)} %pad_maximum_fusion.1), channel_id=1, source_target_pairs={{0,3},{1,2},{2,1},{3,0},{4,7},{5,6},{6,5},{7,4},{8,9},{9,8},{10,11... | collective-permute-start | bytes 1622024 | tf_op jit(solution)/shard_map/ppermute | solution.py:74
  18.8 3.3 %collective-permute-start.4 = (bf16[256,128]{1,0:T(8,128)(2,1)S(1)}, bf16[256,128]{1,0:T(8,128)(2,1)S(1)}, u32[]{:S(2)}, u32[]{:S(2)}) collective-permute-start(bf16[256,128]{1,0:T(8,128)(2,1)S(1)} %get-tuple-element.16), channel_id=1, source_target_pairs={{0,64},{1,65},{2,66},{3,67},{4,68},{5,69},{6,70},{7,71},{8,200},{9... | collective-permute-start | bytes 196616 | tf_op jit(solution)/shard_map/ppermute | solution.py:74
  22.1 2.5 %collective-permute-done.4 = bf16[256,128]{1,0:T(8,128)(2,1)S(1)} collective-permute-done((bf16[256,128]{1,0:T(8,128)(2,1)S(1)}, bf16[256,128]{1,0:T(8,128)(2,1)S(1)}, u32[]{:S(2)}, u32[]{:S(2)}) %collective-permute-start.4) | collective-permute-done | bytes 65568 | tf_op jit(solution)/shard_map/ppermute | solution.py:74
  24.6 5.9 %collective-permute-start.5 = (bf16[2,256,128]{2,1,0:T(8,128)(2,1)S(1)}, bf16[2,256,128]{2,1,0:T(8,128)(2,1)S(1)}, u32[]{:S(2)}, u32[]{:S(2)}) collective-permute-start(bf16[2,256,128]{2,1,0:T(8,128)(2,1)S(1)} %pad_maximum_fusion.5), channel_id=1, source_target_pairs={{0,192},{1,193},{2,194},{3,195},{4,196},{5,197},{6,198},{7,199},{8... | collective-permute-start | bytes 393224 | tf_op jit(solution)/shard_map/ppermute | solution.py:74
  30.5 4.4 %collective-permute-done.5 = bf16[2,256,128]{2,1,0:T(8,128)(2,1)S(1)} collective-permute-done((bf16[2,256,128]{2,1,0:T(8,128)(2,1)S(1)}, bf16[2,256,128]{2,1,0:T(8,128)(2,1)S(1)}, u32[]{:S(2)}, u32[]{:S(2)}) %collective-permute-start.5) | collective-permute-done | bytes 131104 | tf_op jit(solution)/shard_map/ppermute | solution.py:74
  34.9 1.7 %collective-permute-start.6 = (bf16[4,256,128]{2,1,0:T(8,128)(2,1)S(1)}, bf16[4,256,128]{2,1,0:T(8,128)(2,1)S(1)}, u32[]{:S(2)}, u32[]{:S(2)}) collective-permute-start(bf16[4,256,128]{2,1,0:T(8,128)(2,1)S(1)} %pad_maximum_fusion.4), channel_id=1, source_target_pairs={{0,16},{1,17},{2,18},{3,19},{4,20},{5,21},{6,22},{7,23},{8,56},{9,... | collective-permute-start | bytes 786440 | tf_op jit(solution)/shard_map/ppermute | solution.py:74
  36.8 4.6 %collective-permute-done.6 = bf16[4,256,128]{2,1,0:T(8,128)(2,1)S(1)} collective-permute-done((bf16[4,256,128]{2,1,0:T(8,128)(2,1)S(1)}, bf16[4,256,128]{2,1,0:T(8,128)(2,1)S(1)}, u32[]{:S(2)}, u32[]{:S(2)}) %collective-permute-start.6) | collective-permute-done | bytes 262176 | tf_op jit(solution)/shard_map/ppermute | solution.py:74
  41.5 3.0 %collective-permute-start.7 = (bf16[8,256,128]{2,1,0:T(8,128)(2,1)S(1)}, bf16[8,256,128]{2,1,0:T(8,128)(2,1)S(1)}, u32[]{:S(2)}, u32[]{:S(2)}) collective-permute-start(bf16[8,256,128]{2,1,0:T(8,128)(2,1)S(1)} %pad_maximum_fusion.2), channel_id=1, source_target_pairs={{0,48},{1,49},{2,50},{3,51},{4,52},{5,53},{6,54},{7,55},{8,24},{9,... | collective-permute-start | bytes 1572872 | tf_op jit(solution)/shard_map/ppermute | solution.py:74
  44.5 0.7 dynamic-slice_bitcast_fusion.ids_ref
  45.2 2.3 %tiles.1 = (s32[264]{0:T(512)S(1)}, s32[64]{0:T(128)S(1)}, s32[16,8,128]{2,1,0:T(8,128)S(1)}) custom-call(s32[256]{0:T(256)S(1)} %copy-done.6, s32[16]{0:T(128)S(1)} %copy-done.7, s32[32]{0:T(128)S(1)} %dynamic-slice_bitcast_fusion.ids_ref), custom_call_target="tpu_custom_call" | custom-call | tf_op jit(solution)/shard_map/tiles/pallas_call | solution.py:215
  47.6 4.4 %collective-permute-done.7 = bf16[8,256,128]{2,1,0:T(8,128)(2,1)S(1)} collective-permute-done((bf16[8,256,128]{2,1,0:T(8,128)(2,1)S(1)}, bf16[8,256,128]{2,1,0:T(8,128)(2,1)S(1)}, u32[]{:S(2)}, u32[]{:S(2)}) %collective-permute-start.7) | collective-permute-done | bytes 524320 | tf_op jit(solution)/shard_map/ppermute | solution.py:74
  52.0 1.0 copy-done.8
  53.1 7.1 %main.1 = (f32[8,128,256]{2,1,0:T(8,128)S(1)}, f32[8,128,256]{2,1,0:T(8,128)S(1)}, f32[8,256,128]{2,1,0:T(8,128)S(1)}, bf16[8,256,128]{2,1,0:T(8,128)(2,1)S(1)}) custom-call(s32[264]{0:T(512)S(1)} %get-tuple-element.12.list_ref, s32[64]{0:T(128)S(1)} %get-tuple-element.13.base_ref, s32[16,8,128]{2,1,0:T(8,128)S(1)} %get-tuple-element.14.rows_ref, ...), custom_call_target="tpu_custom_call" | custom-call | flops 1000000000 | bytes 10000000 | tf_op jit(solution)/shard_map/main/pallas_call | solution.py:237
  60.2 7.1 %collective-permute-start.12 = (bf16[8,256,128]{2,1,0:T(8,128)(2,1)S(1)}, bf16[8,256,128]{2,1,0:T(8,128)(2,1)S(1)}, u32[]{:S(2)}, u32[]{:S(2)}) collective-permute-start(bf16[8,256,128]{2,1,0:T(8,128)(2,1)S(1)} %get-tuple-element.20), channel_id=1, source_target_pairs={{0,48},{1,49},{2,50},{3,51},{4,52},{5,53},{6,54},{7,55},{8,24},{9,... | collective-permute-start | bytes 1572872 | tf_op jit(solution)/shard_map/ppermute | solution.py:74
  67.3 9.7 %collective-permute-done.12 = bf16[8,256,128]{2,1,0:T(8,128)(2,1)S(1)} collective-permute-done((bf16[8,256,128]{2,1,0:T(8,128)(2,1)S(1)}, bf16[8,256,128]{2,1,0:T(8,128)(2,1)S(1)}, u32[]{:S(2)}, u32[]{:S(2)}) %collective-permute-start.12) | collective-permute-done | bytes 524320 | tf_op jit(solution)/shard_map/ppermute | solution.py:74
  77.1 5.1 %collective-permute-start.13 = (bf16[4,256,128]{2,1,0:T(8,128)(2,1)S(1)}, bf16[4,256,128]{2,1,0:T(8,128)(2,1)S(1)}, u32[]{:S(2)}, u32[]{:S(2)}) collective-permute-start(bf16[4,256,128]{2,1,0:T(8,128)(2,1)S(1)} %slice.88), channel_id=1, source_target_pairs={{0,16},{1,17},{2,18},{3,19},{4,20},{5,21},{6,22},{7,23},{8,56},{9,... | collective-permute-start | bytes 786440 | tf_op jit(solution)/shard_map/ppermute | solution.py:74
  82.2 4.4 %collective-permute-done.13 = bf16[4,256,128]{2,1,0:T(8,128)(2,1)S(1)} collective-permute-done((bf16[4,256,128]{2,1,0:T(8,128)(2,1)S(1)}, bf16[4,256,128]{2,1,0:T(8,128)(2,1)S(1)}, u32[]{:S(2)}, u32[]{:S(2)}) %collective-permute-start.13) | collective-permute-done | bytes 262176 | tf_op jit(solution)/shard_map/ppermute | solution.py:74
  86.7 3.0 %collective-permute-start.14 = (f32[2,256,128]{2,1,0:T(8,128)S(1)}, f32[2,256,128]{2,1,0:T(8,128)S(1)}, u32[]{:S(2)}, u32[]{:S(2)}) collective-permute-start(f32[2,256,128]{2,1,0:T(8,128)S(1)} %slice.68), channel_id=1, source_target_pairs={{0,192},{1,193},{2,194},{3,195},{4,196},{5,197},{6,198},{7,199},{8... | collective-permute-start | bytes 786440 | tf_op jit(solution)/shard_map/ppermute | solution.py:74
  90.0 7.5 %collective-permute-done.14 = f32[2,256,128]{2,1,0:T(8,128)S(1)} collective-permute-done((f32[2,256,128]{2,1,0:T(8,128)S(1)}, f32[2,256,128]{2,1,0:T(8,128)S(1)}, u32[]{:S(2)}, u32[]{:S(2)}) %collective-permute-start.14) | collective-permute-done | bytes 262176 | tf_op jit(solution)/shard_map/ppermute | solution.py:74
  97.5 0.9 collective-permute-start.15
  98.6 6.2 %collective-permute-done.15 = f32[256,128]{1,0:T(8,128)S(1)} collective-permute-done((f32[256,128]{1,0:T(8,128)S(1)}, f32[256,128]{1,0:T(8,128)S(1)}, u32[]{:S(2)}, u32[]{:S(2)}) %collective-permute-start.15) | collective-permute-done | bytes 131104 | tf_op jit(solution)/shard_map/ppermute | solution.py:74
  104.9 4.6 %collective-permute-start.11 = (f32[128,256]{1,0:T(8,128)S(1)}, f32[128,256]{1,0:T(8,128)S(1)}, u32[]{:S(2)}, u32[]{:S(2)}) collective-permute-start(f32[128,256]{1,0:T(8,128)S(1)} %slice_bitcast_fusion.2), channel_id=1, source_target_pairs={{0,4},{1,5},{2,6},{3,7},{4,0},{5,1},{6,2},{7,3},{8,204},{9,205},{1... | collective-permute-start | bytes 393224 | tf_op jit(solution)/shard_map/ppermute | solution.py:74
  110.2 2.3 %collective-permute-done.11 = f32[128,256]{1,0:T(8,128)S(1)} collective-permute-done((f32[128,256]{1,0:T(8,128)S(1)}, f32[128,256]{1,0:T(8,128)S(1)}, u32[]{:S(2)}, u32[]{:S(2)}) %collective-permute-start.11) | collective-permute-done | bytes 131104 | tf_op jit(solution)/shard_map/ppermute | solution.py:74
  (51 shorter events, 3.7 us)
Async XLA Ops:
  0.6 0.8 copy-start
  1.5 0.8 copy-start.1
  2.3 0.8 copy-start.2
  3.2 0.8 copy-start.3
  3.9 0.8 copy-start.4
  4.7 0.7 copy-start.5
  5.5 5.1 %collective-permute-start = (bf16[528,128]{1,0:T(8,128)(2,1)S(1)}, bf16[528,128]{1,0:T(8,128)(2,1)S(1)}, u32[]{:S(2)}, u32[]{:S(2)}) collective-permute-start(bf16[528,128]{1,0:T(8,128)(2,1)S(1)} %get-tuple-element.15), channel_id=1, source_target_pairs={{0,4},{1,5},{2,6},{3,7},{4,0},{5,1},{6,2},{7,3},{8,204},{9,205},{1... | collective-permute-start | bytes 405512 | tf_op jit(solution)/shard_map/ppermute | solution.py:74
  10.6 6.8 %collective-permute-start.1 = (bf16[2,528,128]{2,1,0:T(8,128)(2,1)S(1)}, bf16[2,528,128]{2,1,0:T(8,128)(2,1)S(1)}, u32[]{:S(2)}, u32[]{:S(2)}) collective-permute-start(bf16[2,528,128]{2,1,0:T(8,128)(2,1)S(1)} %pad_maximum_fusion.3), channel_id=1, source_target_pairs={{0,1},{1,0},{2,3},{3,2},{4,5},{5,4},{6,7},{7,6},{8,11},{9,10},{10,... | collective-permute-start | bytes 811016 | tf_op jit(solution)/shard_map/ppermute | solution.py:74
  17.5 19.1 %collective-permute-start.2 = (bf16[4,528,128]{2,1,0:T(8,128)(2,1)S(1)}, bf16[4,528,128]{2,1,0:T(8,128)(2,1)S(1)}, u32[]{:S(2)}, u32[]{:S(2)}) collective-permute-start(bf16[4,528,128]{2,1,0:T(8,128)(2,1)S(1)} %pad_maximum_fusion.1), channel_id=1, source_target_pairs={{0,3},{1,2},{2,1},{3,0},{4,7},{5,6},{6,5},{7,4},{8,9},{9,8},{10,11... | collective-permute-start | bytes 1622024 | tf_op jit(solution)/shard_map/ppermute | solution.py:74
  18.8 5.8 %collective-permute-start.4 = (bf16[256,128]{1,0:T(8,128)(2,1)S(1)}, bf16[256,128]{1,0:T(8,128)(2,1)S(1)}, u32[]{:S(2)}, u32[]{:S(2)}) collective-permute-start(bf16[256,128]{1,0:T(8,128)(2,1)S(1)} %get-tuple-element.16), channel_id=1, source_target_pairs={{0,64},{1,65},{2,66},{3,67},{4,68},{5,69},{6,70},{7,71},{8,200},{9... | collective-permute-start | bytes 196616 | tf_op jit(solution)/shard_map/ppermute | solution.py:74
  24.6 10.2 %collective-permute-start.5 = (bf16[2,256,128]{2,1,0:T(8,128)(2,1)S(1)}, bf16[2,256,128]{2,1,0:T(8,128)(2,1)S(1)}, u32[]{:S(2)}, u32[]{:S(2)}) collective-permute-start(bf16[2,256,128]{2,1,0:T(8,128)(2,1)S(1)} %pad_maximum_fusion.5), channel_id=1, source_target_pairs={{0,192},{1,193},{2,194},{3,195},{4,196},{5,197},{6,198},{7,199},{8... | collective-permute-start | bytes 393224 | tf_op jit(solution)/shard_map/ppermute | solution.py:74
  34.9 6.6 %collective-permute-start.6 = (bf16[4,256,128]{2,1,0:T(8,128)(2,1)S(1)}, bf16[4,256,128]{2,1,0:T(8,128)(2,1)S(1)}, u32[]{:S(2)}, u32[]{:S(2)}) collective-permute-start(bf16[4,256,128]{2,1,0:T(8,128)(2,1)S(1)} %pad_maximum_fusion.4), channel_id=1, source_target_pairs={{0,16},{1,17},{2,18},{3,19},{4,20},{5,21},{6,22},{7,23},{8,56},{9,... | collective-permute-start | bytes 786440 | tf_op jit(solution)/shard_map/ppermute | solution.py:74
  36.6 8.5 %copy-start.6 = (s32[256]{0:T(256)S(1)}, s32[256]{0:T(256)}, u32[]{:S(2)}) copy-start(s32[256]{0:T(256)} %perm_ref.1) | copy-start | bytes 3076
  36.6 8.5 %copy-start.7 = (s32[16]{0:T(128)S(1)}, s32[16]{0:T(128)}, u32[]{:S(2)}) copy-start(s32[16]{0:T(128)} %bounds_ref.1) | copy-start | bytes 196
  36.7 15.4 %collective-permute-start.3 = (bf16[8,528,128]{2,1,0:T(8,128)(2,1)S(1)}, bf16[8,528,128]{2,1,0:T(8,128)(2,1)S(1)}, u32[]{:S(2)}, u32[]{:S(2)}) collective-permute-start(bf16[8,528,128]{2,1,0:T(8,128)(2,1)S(1)} %pad_maximum_fusion.qa_ref), channel_id=1, source_target_pairs={{0,8},{1,9},{2,10},{3,11},{4,12},{5,13},{6,14},{7,15},{8,0},{9,1},... | collective-permute-start | bytes 3244040 | tf_op jit(solution)/shard_map/ppermute | solution.py:74
  41.5 10.5 %collective-permute-start.7 = (bf16[8,256,128]{2,1,0:T(8,128)(2,1)S(1)}, bf16[8,256,128]{2,1,0:T(8,128)(2,1)S(1)}, u32[]{:S(2)}, u32[]{:S(2)}) collective-permute-start(bf16[8,256,128]{2,1,0:T(8,128)(2,1)S(1)} %pad_maximum_fusion.2), channel_id=1, source_target_pairs={{0,48},{1,49},{2,50},{3,51},{4,52},{5,53},{6,54},{7,55},{8,24},{9,... | collective-permute-start | bytes 1572872 | tf_op jit(solution)/shard_map/ppermute | solution.py:74
  52.0 1.0 copy-start.8
  60.2 16.7 %collective-permute-start.12 = (bf16[8,256,128]{2,1,0:T(8,128)(2,1)S(1)}, bf16[8,256,128]{2,1,0:T(8,128)(2,1)S(1)}, u32[]{:S(2)}, u32[]{:S(2)}) collective-permute-start(bf16[8,256,128]{2,1,0:T(8,128)(2,1)S(1)} %get-tuple-element.20), channel_id=1, source_target_pairs={{0,48},{1,49},{2,50},{3,51},{4,52},{5,53},{6,54},{7,55},{8,24},{9,... | collective-permute-start | bytes 1572872 | tf_op jit(solution)/shard_map/ppermute | solution.py:74
  67.3 22.4 %collective-permute-start.8 = (f32[8,128,256]{2,1,0:T(8,128)S(1)}, f32[8,128,256]{2,1,0:T(8,128)S(1)}, u32[]{:S(2)}, u32[]{:S(2)}) collective-permute-start(f32[8,128,256]{2,1,0:T(8,128)S(1)} %get-tuple-element.18), channel_id=1, source_target_pairs={{0,8},{1,9},{2,10},{3,11},{4,12},{5,13},{6,14},{7,15},{8,0},{9,1},... | collective-permute-start | bytes 3145736 | tf_op jit(solution)/shard_map/ppermute | solution.py:74
  77.1 9.5 %collective-permute-start.13 = (bf16[4,256,128]{2,1,0:T(8,128)(2,1)S(1)}, bf16[4,256,128]{2,1,0:T(8,128)(2,1)S(1)}, u32[]{:S(2)}, u32[]{:S(2)}) collective-permute-start(bf16[4,256,128]{2,1,0:T(8,128)(2,1)S(1)} %slice.88), channel_id=1, source_target_pairs={{0,16},{1,17},{2,18},{3,19},{4,20},{5,21},{6,22},{7,23},{8,56},{9,... | collective-permute-start | bytes 786440 | tf_op jit(solution)/shard_map/ppermute | solution.py:74
  86.7 10.8 %collective-permute-start.14 = (f32[2,256,128]{2,1,0:T(8,128)S(1)}, f32[2,256,128]{2,1,0:T(8,128)S(1)}, u32[]{:S(2)}, u32[]{:S(2)}) collective-permute-start(f32[2,256,128]{2,1,0:T(8,128)S(1)} %slice.68), channel_id=1, source_target_pairs={{0,192},{1,193},{2,194},{3,195},{4,196},{5,197},{6,198},{7,199},{8... | collective-permute-start | bytes 786440 | tf_op jit(solution)/shard_map/ppermute | solution.py:74
  89.9 8.5 %collective-permute-start.9 = (bf16[4,128,256]{2,1,0:T(8,128)(2,1)S(1)}, bf16[4,128,256]{2,1,0:T(8,128)(2,1)S(1)}, u32[]{:S(2)}, u32[]{:S(2)}) collective-permute-start(bf16[4,128,256]{2,1,0:T(8,128)(2,1)S(1)} %slice.89), channel_id=1, source_target_pairs={{0,3},{1,2},{2,1},{3,0},{4,7},{5,6},{6,5},{7,4},{8,9},{9,8},{10,11... | collective-permute-start | bytes 786440 | tf_op jit(solution)/shard_map/ppermute | solution.py:74
  97.5 7.3 %collective-permute-start.15 = (f32[256,128]{1,0:T(8,128)S(1)}, f32[256,128]{1,0:T(8,128)S(1)}, u32[]{:S(2)}, u32[]{:S(2)}) collective-permute-start(f32[256,128]{1,0:T(8,128)S(1)} %slice_bitcast_fusion), channel_id=1, source_target_pairs={{0,64},{1,65},{2,66},{3,67},{4,68},{5,69},{6,70},{7,71},{8,200},{9... | collective-permute-start | bytes 393224 | tf_op jit(solution)/shard_map/ppermute | solution.py:74
  98.5 6.3 %collective-permute-start.10 = (bf16[2,128,256]{2,1,0:T(8,128)(2,1)S(1)}, bf16[2,128,256]{2,1,0:T(8,128)(2,1)S(1)}, u32[]{:S(2)}, u32[]{:S(2)}) collective-permute-start(bf16[2,128,256]{2,1,0:T(8,128)(2,1)S(1)} %slice.90), channel_id=1, source_target_pairs={{0,1},{1,0},{2,3},{3,2},{4,5},{5,4},{6,7},{7,6},{8,11},{9,10},{10,... | collective-permute-start | bytes 393224 | tf_op jit(solution)/shard_map/ppermute | solution.py:74
  104.9 7.5 %collective-permute-start.11 = (f32[128,256]{1,0:T(8,128)S(1)}, f32[128,256]{1,0:T(8,128)S(1)}, u32[]{:S(2)}, u32[]{:S(2)}) collective-permute-start(f32[128,256]{1,0:T(8,128)S(1)} %slice_bitcast_fusion.2), channel_id=1, source_target_pairs={{0,4},{1,5},{2,6},{3,7},{4,0},{5,1},{6,2},{7,3},{8,204},{9,205},{1... | collective-permute-start | bytes 393224 | tf_op jit(solution)/shard_map/ppermute | solution.py:74
